TPU v7x, 32 devices: a whole 2x2x4 slice. The times are simulated.
32 devices in a mesh: section: 2 (over core), dp: 4 (over z), tensor: 4 (over y, x).
Axes of the slice: x: 2, y: 2, z: 4, core: 2. Of those that a mesh axis runs over, the one named last changes fastest.
Arguments:
- inputs: bfloat16 [3, 4608, 768], P(None, ('dp', 'tensor')), may hold values from -6 to 6
- cotangent: bfloat16 [3, 4608, 768], P(None, ('dp', 'tensor')), may hold values from -6 to 6
- lengths: int32 [4, 3, 4], P('dp'), may hold values from 1 to 1024, as said below
- ln1_gain: bfloat16 [2, 768], P('section', ('dp', 'tensor')), may hold values from 0.5 to 1.5
- ln1_bias: bfloat16 [2, 768], P('section', ('dp', 'tensor')), may hold values from -1.75 to 1.75
- q_weight: bfloat16 [2, 768, 768], P('section', 'dp', 'tensor'), may hold values from -0.21875 to 0.21875
- q_bias: bfloat16 [2, 12, 64], P('section', 'tensor', 'dp'), may hold values from -3 to 3
- k_weight: bfloat16 [2, 768, 768], P('section', 'dp', 'tensor'), may hold values from -0.21875 to 0.21875
- v_weight: bfloat16 [2, 768, 768], P('section', 'dp', 'tensor'), may hold values from -0.21875 to 0.21875
- v_bias: bfloat16 [2, 12, 64], P('section', 'tensor', 'dp'), may hold values from -3 to 3
- o_weight: bfloat16 [2, 768, 768], P('section', 'tensor', 'dp'), may hold values from -3.5 to 3.5
- o_bias: bfloat16 [2, 768], P('section', ('dp', 'tensor')), may hold values from -1.75 to 1.75
- ln2_gain: bfloat16 [2, 768], P('section', ('dp', 'tensor')), may hold values from 0.5 to 1.5
- ln2_bias: bfloat16 [2, 768], P('section', ('dp', 'tensor')), may hold values from -1.75 to 1.75
- fc1_weight: bfloat16 [2, 768, 3072], P('section', 'dp', 'tensor'), may hold values from -0.21875 to 0.21875
- fc1_bias: bfloat16 [2, 48, 64], P('section', 'tensor', 'dp'), may hold values from -3 to 3
- fc2_weight: bfloat16 [2, 3072, 768], P('section', 'tensor', 'dp'), may hold values from -0.625 to 0.625
- fc2_bias: bfloat16 [2, 768], P('section', ('dp', 'tensor')), may hold values from -1.75 to 1.75
Outputs:
- acts: bfloat16 [2, 3, 4608, 768], P('section', None, ('dp', 'tensor'))
- backs: bfloat16 [2, 3, 4608, 768], P('section', None, ('dp', 'tensor'))
- grad_ln1_gain: float32 [2, 768], P('section', ('dp', 'tensor'))
- grad_ln1_bias: float32 [2, 768], P('section', ('dp', 'tensor'))
- grad_q_weight: float32 [2, 768, 768], P('section', 'dp', 'tensor')
- grad_q_bias: float32 [2, 12, 64], P('section', 'tensor', 'dp')
- grad_k_weight: float32 [2, 768, 768], P('section', 'dp', 'tensor')
- grad_v_weight: float32 [2, 768, 768], P('section', 'dp', 'tensor')
- grad_v_bias: float32 [2, 12, 64], P('section', 'tensor', 'dp')
- grad_o_weight: float32 [2, 768, 768], P('section', 'tensor', 'dp')
- grad_o_bias: float32 [2, 768], P('section', ('dp', 'tensor'))
- grad_ln2_gain: float32 [2, 768], P('section', ('dp', 'tensor'))
- grad_ln2_bias: float32 [2, 768], P('section', ('dp', 'tensor'))
- grad_fc1_weight: float32 [2, 768, 3072], P('section', 'dp', 'tensor')
- grad_fc1_bias: float32 [2, 48, 64], P('section', 'tensor', 'dp')
- grad_fc2_weight: float32 [2, 3072, 768], P('section', 'tensor', 'dp')
- grad_fc2_bias: float32 [2, 768], P('section', ('dp', 'tensor'))
Inputs may be any that keep to these rules, and one draw needn't show every extreme that they name: In each row lengths[g, m], one entry is exactly 1024, at a place that varies; the other entries are positive and sum to 128.
All inputs are finite; a program needn't handle non-finite values.
Results may differ from a plain program's by a relative error of at most 0.018.
Values may be sent and summed in bfloat16 or wider, within the bound.
A program may use at most 256 MiB of HBM per device.

v0:
```python
import jax
import jax.numpy as jnp
from jax import lax
from jax.sharding import PartitionSpec as P

HD = 64
TOK_MB = 1152


EPSILON = 1e-05


def from_behind(array, axis, by):
    peers = lax.axis_size(axis)
    pairs = [(i, i + by) for i in range(peers) if 0 <= i + by < peers]
    return lax.ppermute(array, axis, pairs)


def normalize(values, scale_vec, shift_vec):
    center = values - jnp.mean(values, axis=-1, keepdims=True)
    spread = jnp.mean(center * center, axis=-1, keepdims=True)
    return center * lax.rsqrt(spread + EPSILON) * scale_vec + shift_vec


def plain(left, right):
    return jnp.dot(left, right, preferred_element_type=jnp.float32)


def contract_rows(left, right):
    return lax.dot_general(
        left, right, (((0,), (0,)), ((), ())), preferred_element_type=jnp.float32
    )


def contract_cols(left, right):
    return lax.dot_general(
        left, right, (((1,), (1,)), ((), ())), preferred_element_type=jnp.float32
    )


def doc_mask(length_row, row_count):
    doc_ends = jnp.cumsum(length_row)
    places = jnp.arange(row_count, dtype=jnp.int32)
    doc_ids = jnp.sum((places[:, None] >= doc_ends[None, :]).astype(jnp.int32), axis=1)
    same_doc = doc_ids[:, None] == doc_ids[None, :]
    causal = places[None, :] <= places[:, None]
    return same_doc & causal


def attention_probs(query_heads, key_heads, allowed, score_scale, log_total):
    scores = (
        jnp.einsum("qhd,khd->hqk", query_heads, key_heads, preferred_element_type=jnp.float32)
        * score_scale
    )
    scores = jnp.where(allowed[None], scores, -1e30)
    return jnp.exp(scores - log_total)


def attend(query_heads, key_heads, value_heads, allowed):
    scores = jnp.einsum(
        "qhd,khd->hqk", query_heads, key_heads, preferred_element_type=jnp.float32
    ) * HD ** (-0.5)
    scores = jnp.where(allowed[None], scores, -1e30)
    row_top = jnp.max(scores, axis=-1, keepdims=True)
    exponent = jnp.exp(scores - row_top)
    row_total = jnp.sum(exponent, axis=-1, keepdims=True)
    attention = (exponent / row_total).astype(jnp.bfloat16)
    log_total = row_top + jnp.log(row_total)
    mixed = jnp.einsum("hqk,khd->qhd", attention, value_heads, preferred_element_type=jnp.float32)
    return (mixed, log_total)


def forward_layer(source, allowed, vectors, matrices):
    ln1_gain, ln1_bias, o_bias, ln2_gain, ln2_bias, fc2_bias = vectors
    q_weight, k_weight, v_weight, o_weight, fc1_weight, fc2_weight, q_bias, v_bias, fc1_bias = (
        matrices
    )
    hidden = source.astype(jnp.float32)
    normed = normalize(hidden, ln1_gain, ln1_bias).astype(jnp.bfloat16)
    normed_all = lax.all_gather(normed, "tensor", axis=0, tiled=True)
    row_count = normed_all.shape[0]
    queries = (plain(normed_all, q_weight) + q_bias).astype(jnp.bfloat16)
    key_rows = plain(normed_all, k_weight).astype(jnp.bfloat16)
    values = (plain(normed_all, v_weight) + v_bias).astype(jnp.bfloat16)
    head_local = queries.shape[1] // HD
    mixed, log_total = attend(
        queries.reshape(row_count, head_local, HD),
        key_rows.reshape(row_count, head_local, HD),
        values.reshape(row_count, head_local, HD),
        allowed,
    )
    mixed = mixed.reshape(row_count, head_local * HD).astype(jnp.bfloat16)
    branch = lax.psum_scatter(plain(mixed, o_weight), "tensor", scatter_dimension=0, tiled=True)
    middle = hidden + branch + o_bias
    normed_two = normalize(middle, ln2_gain, ln2_bias).astype(jnp.bfloat16)
    normed_two_all = lax.all_gather(normed_two, "tensor", axis=0, tiled=True)
    hidden_pre = plain(normed_two_all, fc1_weight) + fc1_bias
    active = jax.nn.gelu(hidden_pre, approximate=True).astype(jnp.bfloat16)
    branch_two = lax.psum_scatter(
        plain(active, fc2_weight), "tensor", scatter_dimension=0, tiled=True
    )
    result = middle + branch_two + fc2_bias
    saved = (
        hidden,
        middle,
        normed_all,
        queries,
        key_rows,
        values,
        log_total,
        mixed,
        normed_two_all,
        hidden_pre,
        active,
    )
    return (result.astype(jnp.bfloat16), saved)


def backward_layer(grad_out, allowed, vectors, matrices, saved):
    ln1_gain, ln1_bias, o_bias, ln2_gain, ln2_bias, fc2_bias = vectors
    q_weight, k_weight, v_weight, o_weight, fc1_weight, fc2_weight, q_bias, v_bias, fc1_bias = (
        matrices
    )
    (
        hidden,
        middle,
        normed_all,
        queries,
        key_rows,
        values,
        log_total,
        mixed,
        normed_two_all,
        hidden_pre,
        active,
    ) = saved
    row_count = normed_all.shape[0]
    head_local = queries.shape[1] // HD
    grad_mlp = grad_out.astype(jnp.bfloat16)
    grad_mlp_all = lax.all_gather(grad_mlp, "tensor", axis=0, tiled=True)
    grad_fc2 = contract_rows(active, grad_mlp_all)
    grad_fc2_bias = jnp.sum(grad_out, axis=0)
    grad_active = contract_cols(grad_mlp_all, fc2_weight)
    gelu_value, gelu_pull = jax.vjp(lambda inner: jax.nn.gelu(inner, approximate=True), hidden_pre)
    grad_pre = gelu_pull(grad_active)[0].astype(jnp.bfloat16)
    grad_fc1_bias = jnp.sum(grad_pre, axis=0, dtype=jnp.float32)
    grad_fc1 = contract_rows(normed_two_all, grad_pre)
    grad_normed_two = lax.psum_scatter(
        contract_cols(grad_pre, fc1_weight), "tensor", scatter_dimension=0, tiled=True
    )
    norm_value, norm_pull = jax.vjp(normalize, middle, ln2_gain, ln2_bias)
    grad_middle, grad_ln2_gain, grad_ln2_bias = norm_pull(grad_normed_two)
    grad_middle = grad_middle + grad_out
    grad_o_bias = jnp.sum(grad_middle, axis=0)
    grad_branch = grad_middle.astype(jnp.bfloat16)
    grad_branch_all = lax.all_gather(grad_branch, "tensor", axis=0, tiled=True)
    grad_o = contract_rows(mixed, grad_branch_all)
    grad_mixed = contract_cols(grad_branch_all, o_weight).astype(jnp.bfloat16)
    query_heads = queries.reshape(row_count, head_local, HD)
    key_heads = key_rows.reshape(row_count, head_local, HD)
    value_heads = values.reshape(row_count, head_local, HD)
    grad_heads = grad_mixed.reshape(row_count, head_local, HD)
    score_scale = HD ** (-0.5)
    attention = attention_probs(query_heads, key_heads, allowed, score_scale, log_total)
    grad_probs = jnp.einsum(
        "qhd,khd->hqk", grad_heads, value_heads, preferred_element_type=jnp.float32
    )
    grad_values = jnp.einsum(
        "hqk,qhd->khd",
        attention.astype(jnp.bfloat16),
        grad_heads,
        preferred_element_type=jnp.float32,
    )
    grad_values = grad_values.reshape(row_count, head_local * HD).astype(jnp.bfloat16)
    row_delta = jnp.sum(attention * grad_probs, axis=-1, keepdims=True)
    grad_scores = (attention * (grad_probs - row_delta)).astype(jnp.bfloat16)
    grad_queries = (
        jnp.einsum("hqk,khd->qhd", grad_scores, key_heads, preferred_element_type=jnp.float32)
        * score_scale
    )
    grad_queries = grad_queries.reshape(row_count, head_local * HD).astype(jnp.bfloat16)
    grad_keys = (
        jnp.einsum("hqk,qhd->khd", grad_scores, query_heads, preferred_element_type=jnp.float32)
        * score_scale
    )
    grad_keys = grad_keys.reshape(row_count, head_local * HD).astype(jnp.bfloat16)
    grad_q_bias = jnp.sum(grad_queries, axis=0, dtype=jnp.float32)
    grad_v_bias = jnp.sum(grad_values, axis=0, dtype=jnp.float32)
    grad_qw = contract_rows(normed_all, grad_queries)
    grad_kw = contract_rows(normed_all, grad_keys)
    grad_vw = contract_rows(normed_all, grad_values)
    grad_normed_part = contract_cols(grad_queries, q_weight) + contract_cols(grad_keys, k_weight)
    grad_normed_part = grad_normed_part + contract_cols(grad_values, v_weight)
    grad_normed = lax.psum_scatter(grad_normed_part, "tensor", scatter_dimension=0, tiled=True)
    first_value, first_pull = jax.vjp(normalize, hidden, ln1_gain, ln1_bias)
    grad_hidden, grad_ln1_gain, grad_ln1_bias = first_pull(grad_normed)
    grad_hidden = grad_hidden + grad_middle
    vector_terms = (
        grad_ln1_gain,
        grad_ln1_bias,
        grad_o_bias,
        grad_ln2_gain,
        grad_ln2_bias,
        grad_fc2_bias,
    )
    matrix_terms = (
        grad_qw,
        grad_kw,
        grad_vw,
        grad_o,
        grad_fc1,
        grad_fc2,
        grad_q_bias,
        grad_v_bias,
        grad_fc1_bias,
    )
    return (grad_hidden.astype(jnp.bfloat16), vector_terms, matrix_terms)


def local(
    inputs,
    cotangent,
    lengths,
    ln1_gain,
    ln1_bias,
    q_weight,
    q_bias,
    k_weight,
    v_weight,
    v_bias,
    o_weight,
    o_bias,
    ln2_gain,
    ln2_bias,
    fc1_weight,
    fc1_bias,
    fc2_weight,
    fc2_bias,
):
    section_index = lax.axis_index("section")
    micro_count = inputs.shape[0]
    vector_parts = (
        lax.all_gather(ln1_gain, ("dp", "tensor"), axis=1, tiled=True),
        lax.all_gather(ln1_bias, ("dp", "tensor"), axis=1, tiled=True),
        lax.all_gather(o_bias, ("dp", "tensor"), axis=1, tiled=True),
        lax.all_gather(ln2_gain, ("dp", "tensor"), axis=1, tiled=True),
        lax.all_gather(ln2_bias, ("dp", "tensor"), axis=1, tiled=True),
        lax.all_gather(fc2_bias, ("dp", "tensor"), axis=1, tiled=True),
    )
    vectors = tuple((element[0].astype(jnp.float32) for element in vector_parts))

    def fetch_weights():
        gathered = (
            lax.all_gather(q_weight, "dp", axis=1, tiled=True),
            lax.all_gather(k_weight, "dp", axis=1, tiled=True),
            lax.all_gather(v_weight, "dp", axis=1, tiled=True),
            lax.all_gather(o_weight, "dp", axis=2, tiled=True),
            lax.all_gather(fc1_weight, "dp", axis=1, tiled=True),
            lax.all_gather(fc2_weight, "dp", axis=2, tiled=True),
            lax.all_gather(q_bias, "dp", axis=2, tiled=True),
            lax.all_gather(v_bias, "dp", axis=2, tiled=True),
            lax.all_gather(fc1_bias, "dp", axis=2, tiled=True),
        )
        return tuple((element[0] for element in gathered[:6])) + tuple(
            (element[0].reshape(-1) for element in gathered[6:])
        )

    def allowed_for(batch_index):
        length_row = lax.dynamic_index_in_dim(lengths[0], batch_index, 0, keepdims=False)
        return doc_mask(length_row, TOK_MB)

    received = jnp.zeros(inputs.shape[1:], jnp.bfloat16)
    result_list = []
    saved_list = []
    for moment in range(micro_count + 1):
        batch_index = jnp.clip(moment - section_index, 0, micro_count - 1)
        source = jnp.where(section_index == 0, inputs[min(moment, micro_count - 1)], received)
        matrices = fetch_weights()
        result, saved = forward_layer(source, allowed_for(batch_index), vectors, matrices)
        received = from_behind(result, "section", 1)
        result_list.append(result)
        saved_list.append(saved)
    acts = jnp.stack(
        [
            jnp.where(section_index == 0, result_list[moment], result_list[moment + 1])
            for moment in range(micro_count)
        ]
    )[None]
    saved_stack = jax.tree.map(lambda *elements: jnp.stack(elements), *saved_list)
    vector_totals = tuple((jnp.zeros(element.shape, jnp.float32) for element in vectors))
    matrix_totals = None
    sent_back = jnp.zeros(inputs.shape[1:], jnp.bfloat16)
    back_list = []
    for moment in range(micro_count + 1):
        batch_index = moment - 1 + section_index
        valid_flag = ((batch_index >= 0) & (batch_index < micro_count)).astype(jnp.float32)
        clipped = jnp.clip(batch_index, 0, micro_count - 1)
        forward_turn = jnp.clip(batch_index + section_index, 0, micro_count)
        saved = jax.tree.map(
            lambda element: lax.dynamic_index_in_dim(element, forward_turn, 0, keepdims=False),
            saved_stack,
        )
        given = lax.dynamic_index_in_dim(cotangent, clipped, 0, keepdims=False)
        grad_top = jnp.where(section_index == 1, given, sent_back).astype(jnp.float32) * valid_flag
        matrices = fetch_weights()
        grad_input, vector_terms, matrix_terms = backward_layer(
            grad_top, allowed_for(clipped), vectors, matrices, saved
        )
        sent_back = from_behind(grad_input, "section", -1)
        back_list.append(grad_input)
        vector_totals = tuple((left + right for left, right in zip(vector_totals, vector_terms)))
        if matrix_totals is None:
            matrix_totals = matrix_terms
        else:
            matrix_totals = tuple(
                (left + right for left, right in zip(matrix_totals, matrix_terms))
            )
    backs = jnp.stack(
        [
            jnp.where(section_index == 0, back_list[moment + 1], back_list[moment])
            for moment in range(micro_count)
        ]
    )[None]
    (
        grad_qw,
        grad_kw,
        grad_vw,
        grad_o,
        grad_fc1,
        grad_fc2,
        grad_q_bias,
        grad_v_bias,
        grad_fc1_bias,
    ) = matrix_totals
    summed = (
        lax.psum_scatter(grad_qw[None], "dp", scatter_dimension=1, tiled=True),
        lax.psum_scatter(grad_kw[None], "dp", scatter_dimension=1, tiled=True),
        lax.psum_scatter(grad_vw[None], "dp", scatter_dimension=1, tiled=True),
        lax.psum_scatter(grad_o[None], "dp", scatter_dimension=2, tiled=True),
        lax.psum_scatter(grad_fc1[None], "dp", scatter_dimension=1, tiled=True),
        lax.psum_scatter(grad_fc2[None], "dp", scatter_dimension=2, tiled=True),
        lax.psum_scatter(grad_q_bias.reshape(1, -1, HD), "dp", scatter_dimension=2, tiled=True),
        lax.psum_scatter(grad_v_bias.reshape(1, -1, HD), "dp", scatter_dimension=2, tiled=True),
        lax.psum_scatter(grad_fc1_bias.reshape(1, -1, HD), "dp", scatter_dimension=2, tiled=True),
    )
    vector_sums = (
        lax.psum_scatter(vector_totals[0][None], ("dp", "tensor"), scatter_dimension=1, tiled=True),
        lax.psum_scatter(vector_totals[1][None], ("dp", "tensor"), scatter_dimension=1, tiled=True),
        lax.psum_scatter(vector_totals[2][None], ("dp", "tensor"), scatter_dimension=1, tiled=True),
        lax.psum_scatter(vector_totals[3][None], ("dp", "tensor"), scatter_dimension=1, tiled=True),
        lax.psum_scatter(vector_totals[4][None], ("dp", "tensor"), scatter_dimension=1, tiled=True),
        lax.psum_scatter(vector_totals[5][None], ("dp", "tensor"), scatter_dimension=1, tiled=True),
    )
    return (
        acts,
        backs,
        vector_sums[0],
        vector_sums[1],
        summed[0],
        summed[6],
        summed[1],
        summed[2],
        summed[7],
        summed[3],
        vector_sums[2],
        vector_sums[3],
        vector_sums[4],
        summed[4],
        summed[8],
        summed[5],
        vector_sums[5],
    )


def solution(mesh):
    return jax.shard_map(
        local,
        mesh=mesh,
        in_specs=(
            P(None, ("dp", "tensor"), None),
            P(None, ("dp", "tensor"), None),
            P("dp", None, None),
            P("section", ("dp", "tensor")),
            P("section", ("dp", "tensor")),
            P("section", "dp", "tensor"),
            P("section", "tensor", "dp"),
            P("section", "dp", "tensor"),
            P("section", "dp", "tensor"),
            P("section", "tensor", "dp"),
            P("section", "tensor", "dp"),
            P("section", ("dp", "tensor")),
            P("section", ("dp", "tensor")),
            P("section", ("dp", "tensor")),
            P("section", "dp", "tensor"),
            P("section", "tensor", "dp"),
            P("section", "tensor", "dp"),
            P("section", ("dp", "tensor")),
        ),
        out_specs=(
            P("section", None, ("dp", "tensor"), None),
            P("section", None, ("dp", "tensor"), None),
            P("section", ("dp", "tensor")),
            P("section", ("dp", "tensor")),
            P("section", "dp", "tensor"),
            P("section", "tensor", "dp"),
            P("section", "dp", "tensor"),
            P("section", "dp", "tensor"),
            P("section", "tensor", "dp"),
            P("section", "tensor", "dp"),
            P("section", ("dp", "tensor")),
            P("section", ("dp", "tensor")),
            P("section", ("dp", "tensor")),
            P("section", "dp", "tensor"),
            P("section", "tensor", "dp"),
            P("section", "tensor", "dp"),
            P("section", ("dp", "tensor")),
        ),
        check_vma=False,
    )
```

profile of v0, /device:TPU:0, one launch (start us, length us, event | category | flops | bytes accessed | tf_op | source)
XLA Modules:
  0.0 2966.9 jit_solution(16493147182225506453)
XLA Ops:
  17.6 78.6 %all-reduce.7 = (bf16[768]{0:T(1024)(128)(2,1)S(1)}, bf16[768]{0:T(1024)(128)(2,1)S(1)}, bf16[768]{0:T(1024)(128)(2,1)S(1)}, bf16[768]{0:T(1024)(128)(2,1)S(1)},...) all-reduce(bf16[768]{0:T(1024)(128)(2,1)S(1)} %dynamic-update-slice, ...), channel_id=1, replica_groups=mesh['section'=2,'dp'=4,'tensor'=4] {'dp','tensor'}, use_global_device_ids=true, to_apply=%add.1 | all-reduce | flops 4608 | bytes 18432
  224.6 44.1 %reduce-scatter.57.cloned.1.call-done = f32[288,768]{1,0:T(8,128)} async-done(((f32[1152,768]{1,0:T(8,128)}), f32[288,768]{1,0:T(8,128)}) %reduce-scatter.57.cloned.1.call-update) | async-done | bytes 884752 | tf_op jit(solution)/shard_map/reduce_scatter | solution.py:93
  342.1 46.3 %reduce-scatter.59.cloned.1.call-done = f32[288,768]{1,0:T(8,128)} async-done(((f32[1152,768]{1,0:T(8,128)}), f32[288,768]{1,0:T(8,128)}) %reduce-scatter.59.cloned.1.call-update) | async-done | bytes 884752 | tf_op jit(solution)/shard_map/reduce_scatter | solution.py:99
  462.0 47.3 %reduce-scatter.61.cloned.1.call-done = f32[288,768]{1,0:T(8,128)} async-done(((f32[1152,768]{1,0:T(8,128)}), f32[288,768]{1,0:T(8,128)}) %reduce-scatter.61.cloned.1.call-update) | async-done | bytes 884752 | tf_op jit(solution)/shard_map/reduce_scatter | solution.py:93
  553.8 47.1 %reduce-scatter.63.cloned.1.call-done = f32[288,768]{1,0:T(8,128)} async-done(((f32[1152,768]{1,0:T(8,128)}), f32[288,768]{1,0:T(8,128)}) %reduce-scatter.63.cloned.1.call-update) | async-done | bytes 884752 | tf_op jit(solution)/shard_map/reduce_scatter | solution.py:99
  675.3 47.3 %reduce-scatter.65.cloned.1.call-done = f32[288,768]{1,0:T(8,128)} async-done(((f32[1152,768]{1,0:T(8,128)}), f32[288,768]{1,0:T(8,128)}) %reduce-scatter.65.cloned.1.call-update) | async-done | bytes 884752 | tf_op jit(solution)/shard_map/reduce_scatter | solution.py:93
  767.1 47.1 %reduce-scatter.67.cloned.1.call-done = f32[288,768]{1,0:T(8,128)} async-done(((f32[1152,768]{1,0:T(8,128)}), f32[288,768]{1,0:T(8,128)}) %reduce-scatter.67.cloned.1.call-update) | async-done | bytes 884752 | tf_op jit(solution)/shard_map/reduce_scatter | solution.py:99
  888.4 47.3 %reduce-scatter.69.cloned.1.call-done = f32[288,768]{1,0:T(8,128)} async-done(((f32[1152,768]{1,0:T(8,128)}), f32[288,768]{1,0:T(8,128)}) %reduce-scatter.69.cloned.1.call-update) | async-done | bytes 884752 | tf_op jit(solution)/shard_map/reduce_scatter | solution.py:93
  1026.1 38.3 %reduce-scatter.73.cloned.1.call-done = f32[288,768]{1,0:T(8,128)} async-done(((f32[1152,768]{1,0:T(8,128)}), f32[288,768]{1,0:T(8,128)}) %reduce-scatter.73.cloned.1.call-update) | async-done | bytes 884752 | tf_op jit(solution)/shard_map/reduce_scatter | solution.py:148
  1158.7 43.9 %reduce-scatter.75.cloned.1.call-done = f32[288,768]{1,0:T(8,128)} async-done(((f32[1152,768]{1,0:T(8,128)}), f32[288,768]{1,0:T(8,128)}) %reduce-scatter.75.cloned.1.call-update) | async-done | bytes 884752 | tf_op jit(solution)/shard_map/reduce_scatter | solution.py:194
  1215.0 32.5 %all-gather.43.cloned.1.call-done = bf16[1152,768]{1,0:T(8,128)(2,1)} async-done(((bf16[288,768]{1,0:T(8,128)(2,1)}), bf16[1152,768]{1,0:T(8,128)(2,1)}) %all-gather.43.cloned.1.call-update) | async-done | bytes 1769488 | tf_op jit(solution)/shard_map/all_gather | solution.py:140
  1261.7 44.2 %reduce-scatter.77.cloned.1.call-done = f32[288,768]{1,0:T(8,128)} async-done(((f32[1152,768]{1,0:T(8,128)}), f32[288,768]{1,0:T(8,128)}) %reduce-scatter.77.cloned.1.call-update) | async-done | bytes 884752 | tf_op jit(solution)/shard_map/reduce_scatter | solution.py:148
  1400.0 43.5 %reduce-scatter.79.cloned.1.call-done = f32[288,768]{1,0:T(8,128)} async-done(((f32[1152,768]{1,0:T(8,128)}), f32[288,768]{1,0:T(8,128)}) %reduce-scatter.79.cloned.1.call-update) | async-done | bytes 884752 | tf_op jit(solution)/shard_map/reduce_scatter | solution.py:194
  1500.9 45.7 %reduce-scatter.81.cloned.1.call-done = f32[288,768]{1,0:T(8,128)} async-done(((f32[1152,768]{1,0:T(8,128)}), f32[288,768]{1,0:T(8,128)}) %reduce-scatter.81.cloned.1.call-update) | async-done | bytes 884752 | tf_op jit(solution)/shard_map/reduce_scatter | solution.py:148
  1638.5 45.7 %reduce-scatter.83.cloned.1.call-done = f32[288,768]{1,0:T(8,128)} async-done(((f32[1152,768]{1,0:T(8,128)}), f32[288,768]{1,0:T(8,128)}) %reduce-scatter.83.cloned.1.call-update) | async-done | bytes 884752 | tf_op jit(solution)/shard_map/reduce_scatter | solution.py:194
  1696.5 32.5 %all-gather.51.cloned.1.call-done = bf16[1152,768]{1,0:T(8,128)(2,1)} async-done(((bf16[288,768]{1,0:T(8,128)(2,1)}), bf16[1152,768]{1,0:T(8,128)(2,1)}) %all-gather.51.cloned.1.call-update) | async-done | bytes 1769488 | tf_op jit(solution)/shard_map/all_gather | solution.py:140
  1741.5 46.0 %reduce-scatter.85.cloned.1.call-done = f32[288,768]{1,0:T(8,128)} async-done(((f32[1152,768]{1,0:T(8,128)}), f32[288,768]{1,0:T(8,128)}) %reduce-scatter.85.cloned.1.call-update) | async-done | bytes 884752 | tf_op jit(solution)/shard_map/reduce_scatter | solution.py:148
  2022.0 119.8 %reduce-scatter.109.cloned.1.call-done = f32[48,1]{1,0:T(8,128)} async-done(((f32[768,1]{1,0:T(8,128)}), f32[48,1]{1,0:T(8,128)}) %reduce-scatter.109.cloned.1.call-update) | async-done | bytes 208
  2143.1 123.9 %reduce-scatter.111.cloned.1.call-done = f32[48,1]{1,0:T(8,128)} async-done(((f32[768,1]{1,0:T(8,128)}), f32[48,1]{1,0:T(8,128)}) %reduce-scatter.111.cloned.1.call-update) | async-done | bytes 208
  2268.3 124.7 %reduce-scatter.115.cloned.1.call-done = f32[48,1]{1,0:T(8,128)} async-done(((f32[768,1]{1,0:T(8,128)}), f32[48,1]{1,0:T(8,128)}) %reduce-scatter.115.cloned.1.call-update) | async-done | bytes 208
  2394.3 124.1 %reduce-scatter.107.cloned.1.call-done = f32[48,1]{1,0:T(8,128)} async-done(((f32[768,1]{1,0:T(8,128)}), f32[48,1]{1,0:T(8,128)}) %reduce-scatter.107.cloned.1.call-update) | async-done | bytes 208
  2663.5 120.4 %reduce-scatter.91.cloned.1.call-done = f32[48,1]{1,0:T(8,128)} async-done(((f32[768,1]{1,0:T(8,128)}), f32[48,1]{1,0:T(8,128)}) %reduce-scatter.91.cloned.1.call-update) | async-done | bytes 208
  2785.2 123.9 %reduce-scatter.93.cloned.1.call-done = f32[48,1]{1,0:T(8,128)} async-done(((f32[768,1]{1,0:T(8,128)}), f32[48,1]{1,0:T(8,128)}) %reduce-scatter.93.cloned.1.call-update) | async-done | bytes 208
  2910.4 48.8 %reduce-scatter.89.cloned.1.call-done = f32[1,192,768]{2,1,0:T(8,128)} async-done(((f32[1,768,768]{2,1,0:T(8,128)}), f32[1,192,768]{2,1,0:T(8,128)}) %reduce-scatter.89.cloned.1.call-update) | async-done | bytes 589840 | tf_op jit(solution)/shard_map/reduce_scatter | solution.py:340
  (1025 shorter events, 1382.9 us)
Async XLA Ops:
  8.1 183.0 %all-gather.19.cloned.1.call-start = ((), (), s32[]{:S(2)}) async-start(), calls=%async_computation.30 | async-start | bytes 2211840 | tf_op jit(solution)/shard_map/all_gather | solution.py:80
  98.2 170.5 %reduce-scatter.57.cloned.1.call-start = ((), (), s32[]{:S(2)}) async-start(), calls=%async_computation.31 | async-start | bytes 4423680 | tf_op jit(solution)/shard_map/reduce_scatter | solution.py:93
  272.1 116.3 %reduce-scatter.59.cloned.1.call-start = ((), (), s32[]{:S(2)}) async-start(), calls=%async_computation.35 | async-start | bytes 4423680 | tf_op jit(solution)/shard_map/reduce_scatter | solution.py:99
  941.1 123.2 %reduce-scatter.73.cloned.1.call-start = ((), (), s32[]{:S(2)}) async-start(), calls=%async_computation.49 | async-start | bytes 4423680 | tf_op jit(solution)/shard_map/reduce_scatter | solution.py:148
  1071.8 130.7 %reduce-scatter.75.cloned.1.call-start = ((), (), s32[]{:S(2)}) async-start(), calls=%async_computation.51 | async-start | bytes 4423680 | tf_op jit(solution)/shard_map/reduce_scatter | solution.py:194
  1312.8 130.7 %reduce-scatter.79.cloned.1.call-start = ((), (), s32[]{:S(2)}) async-start(), calls=%async_computation.55 | async-start | bytes 4423680 | tf_op jit(solution)/shard_map/reduce_scatter | solution.py:194
  1553.6 130.7 %reduce-scatter.83.cloned.1.call-start = ((), (), s32[]{:S(2)}) async-start(), calls=%async_computation.59 | async-start | bytes 4423680 | tf_op jit(solution)/shard_map/reduce_scatter | solution.py:194
  1793.2 191.0 %reduce-scatter.87.cloned.1.call-start = ((), (), s32[]{:S(2)}) async-start(), calls=%async_computation.63 | async-start | bytes 4423680 | tf_op jit(solution)/shard_map/reduce_scatter | solution.py:194
  1875.9 123.4 %reduce-scatter.71.cloned.1.call-start = ((), (), s32[]{:S(2)}) async-start(), calls=%async_computation.47 | async-start | bytes 4423680 | tf_op jit(solution)/shard_map/reduce_scatter | solution.py:99
  1883.2 133.3 %reduce-scatter.113.cloned.1.call-start = ((), (), s32[]{:S(2)}) async-start(), calls=%async_computation.76 | async-start | bytes 40960
  1903.4 116.2 %all-reduce.10.cloned.1.call-start = ((), (), s32[]{:S(2)}) async-start(), calls=%async_computation.78 | async-start | bytes 4718592
  1918.9 222.8 %reduce-scatter.109.cloned.1.call-start = ((), (), s32[]{:S(2)}) async-start(), calls=%async_computation.74 | async-start | bytes 417792
  1928.8 338.2 %reduce-scatter.111.cloned.1.call-start = ((), (), s32[]{:S(2)}) async-start(), calls=%async_computation.75 | async-start | bytes 417792
  1929.8 463.2 %reduce-scatter.115.cloned.1.call-start = ((), (), s32[]{:S(2)}) async-start(), calls=%async_computation.77 | async-start | bytes 417792
  1930.8 587.6 %reduce-scatter.107.cloned.1.call-start = ((), (), s32[]{:S(2)}) async-start(), calls=%async_computation.73 | async-start | bytes 417792
  1931.9 607.5 %reduce-scatter.97.cloned.1.call-start = ((), (), s32[]{:S(2)}) async-start(), calls=%async_computation.68 | async-start | bytes 40960
  1933.1 626.0 %reduce-scatter.103.cloned.1.call-start = ((), (), s32[]{:S(2)}) async-start(), calls=%async_computation.71 | async-start | bytes 40960
  1933.9 649.0 %reduce-scatter.105.cloned.1.call-start = ((), (), s32[]{:S(2)}) async-start(), calls=%async_computation.72 | async-start | bytes 983040
  1937.1 670.7 %reduce-scatter.95.cloned.1.call-start = ((), (), s32[]{:S(2)}) async-start(), calls=%async_computation.67 | async-start | bytes 983040
  1948.8 683.9 %reduce-scatter.99.cloned.1.call-start = ((), (), s32[]{:S(2)}) async-start(), calls=%async_computation.69 | async-start | bytes 983040
  1964.0 693.7 %reduce-scatter.101.cloned.1.call-start = ((), (), s32[]{:S(2)}) async-start(), calls=%async_computation.70 | async-start | bytes 983040
  1974.4 809.5 %reduce-scatter.91.cloned.1.call-start = ((), (), s32[]{:S(2)}) async-start(), calls=%async_computation.65 | async-start | bytes 417792
  1988.0 921.1 %reduce-scatter.93.cloned.1.call-start = ((), (), s32[]{:S(2)}) async-start(), calls=%async_computation.66 | async-start | bytes 417792
  1989.7 969.5 %reduce-scatter.89.cloned.1.call-start = ((), (), s32[]{:S(2)}) async-start(), calls=%async_computation.64 | async-start | bytes 2949120 | tf_op jit(solution)/shard_map/reduce_scatter | solution.py:340
  (292 other events, 9294.4 us)
Sparse Core Ops, SparseCore 0:
  224.1 44.6 reduce-scatter.56
  396.4 32.6 all-gather.26
  462.0 47.2 reduce-scatter.60
  609.7 32.6 all-gather.30
  675.4 47.2 reduce-scatter.64
  822.0 32.6 all-gather.34
  888.5 47.2 reduce-scatter.68
  1071.9 32.5 all-gather.40
  1155.3 47.2 reduce-scatter.74
  1312.9 32.5 all-gather.44
  1396.2 47.2 reduce-scatter.78
  1553.7 32.5 all-gather.48
  1637.0 47.2 reduce-scatter.82
  1793.3 32.5 all-gather.52
  1876.1 47.2 reduce-scatter.86
  1926.2 47.2 reduce-scatter.70
  1976.2 40.3 reduce-scatter.112
  2021.9 119.8 reduce-scatter.108
  2146.3 120.6 reduce-scatter.110
  2272.3 120.6 reduce-scatter.114
  2397.7 120.6 reduce-scatter.106
  2663.1 120.7 reduce-scatter.90
  2788.4 120.6 reduce-scatter.92
  2912.1 47.0 reduce-scatter.88
  (7 shorter events, 152.3 us)
Sparse Core Ops, SparseCore 1:
  226.0 27.5 all-gather.22
  271.6 32.4 all-gather.20
  305.5 30.2 all-gather.24
  342.1 46.3 reduce-scatter.58
  512.1 32.4 all-gather.28
  553.8 47.0 reduce-scatter.62
  725.4 32.4 all-gather.32
  767.1 47.0 reduce-scatter.66
  938.5 32.4 all-gather.36
  973.4 32.4 all-gather.38
  1017.3 47.0 reduce-scatter.72
  1215.1 32.4 all-gather.42
  1258.9 47.0 reduce-scatter.76
  1455.6 32.4 all-gather.46
  1499.5 47.0 reduce-scatter.80
  1696.5 32.4 all-gather.50
  1740.4 47.0 reduce-scatter.84
  1919.0 95.3 all-reduce.9
where the time goes:
time: 2970 us
  waiting for transfers between devices  2040 us (69%)
  matrix products  406 us (14%)
  other arithmetic  210 us (7%)
  blocking collectives  178 us (6%)
  local copies, waits for them, and re-layouts  98.2 us (3%)
    unnamed x63, waiting for transfers between devices  877 us
    reduce_scatter x4, waiting for transfers between devices, forward_layer(): lax.psum_scatter(plain(mixed, o_weight), 'tensor', scatter_dimension=0, t...  186 us
    reduce_scatter x4, waiting for transfers between devices, backward_layer(): lax.psum_scatter(contract_cols(grad_pre, fc1_weight), 'tensor', scatter_d...  174 us
    reduce_scatter x4, waiting for transfers between devices, forward_layer(): lax.psum_scatter(plain(active, fc2_weight), 'tensor', scatter_dimension=0...  141 us
    reduce_scatter x4, waiting for transfers between devices, backward_layer(): lax.psum_scatter(grad_normed_part, 'tensor', scatter_dimension=0, tiled=T...  133 us
    all_gather x4, waiting for transfers between devices, backward_layer(): grad_mlp_all = lax.all_gather(grad_mlp, 'tensor', axis=0, tiled=True)  121 us
    all_gather x4, waiting for transfers between devices, backward_layer(): grad_branch_all = lax.all_gather(grad_branch, 'tensor', axis=0, tiled=True)  117 us
    all_gather x4, waiting for transfers between devices, forward_layer(): normed_two_all = lax.all_gather(normed_two, 'tensor', axis=0, tiled=True)  113 us
  transfers between devices with their start and end apart: 55, of which 50 were waited for; matrix products, arithmetic and copies ran while one was open for 7% of the time, Pallas kernels for 0%

commit v1 on v0

v1 whole, which is shorter than its diff:
```python
import jax
import jax.numpy as jnp
from jax import lax
from jax.sharding import PartitionSpec as P

HD = 64
EPSILON = 1e-05
MASKED = -1e30
ALL = ("dp", "tensor")


def swap(array):
    return lax.ppermute(array, "section", [(0, 1), (1, 0)])


def normalize(values, scale_vec, shift_vec):
    center = values - jnp.mean(values, axis=-1, keepdims=True)
    spread = jnp.mean(center * center, axis=-1, keepdims=True)
    return center * lax.rsqrt(spread + EPSILON) * scale_vec + shift_vec


def plain(left, right):
    return jnp.dot(left, right, preferred_element_type=jnp.float32)


def contract_rows(left, right):
    return lax.dot_general(
        left, right, (((0,), (0,)), ((), ())), preferred_element_type=jnp.float32
    )


def contract_cols(left, right):
    return lax.dot_general(
        left, right, (((1,), (1,)), ((), ())), preferred_element_type=jnp.float32
    )


def heads_of(array):
    return array.reshape(array.shape[0], -1, HD)


def scores_of(queries, keys, rows):
    starts, places, key_places = rows
    scores = jnp.einsum(
        "qhd,khd->hqk", heads_of(queries), heads_of(keys), preferred_element_type=jnp.float32
    ) * HD ** (-0.5)
    allowed = (key_places >= starts) & (key_places <= places)
    return jnp.where(allowed[None], scores, MASKED)


def attend(queries, keys, values, rows):
    scores = scores_of(queries, keys, rows)
    row_top = jnp.max(scores, axis=-1, keepdims=True)
    exponent = jnp.exp(scores - row_top)
    row_total = jnp.sum(exponent, axis=-1, keepdims=True)
    probs = (exponent / row_total).astype(jnp.bfloat16)
    mixed = jnp.einsum("hqk,khd->qhd", probs, heads_of(values), preferred_element_type=jnp.float32)
    return mixed.reshape(queries.shape).astype(jnp.bfloat16), row_top + jnp.log(row_total)


def attend_back(queries, keys, values, rows, log_total, grad_mixed):
    probs = jnp.exp(scores_of(queries, keys, rows) - log_total)
    grads = heads_of(grad_mixed)
    grad_probs = jnp.einsum(
        "qhd,khd->hqk", grads, heads_of(values), preferred_element_type=jnp.float32
    )
    grad_values = jnp.einsum(
        "hqk,qhd->khd", probs.astype(jnp.bfloat16), grads, preferred_element_type=jnp.float32
    )
    row_delta = jnp.sum(probs * grad_probs, axis=-1, keepdims=True)
    grad_scores = (probs * (grad_probs - row_delta)).astype(jnp.bfloat16)
    grad_queries = (
        jnp.einsum("hqk,khd->qhd", grad_scores, heads_of(keys), preferred_element_type=jnp.float32)
        * HD ** (-0.5)
    )
    grad_keys = (
        jnp.einsum(
            "hqk,qhd->khd", grad_scores, heads_of(queries), preferred_element_type=jnp.float32
        )
        * HD ** (-0.5)
    )
    return tuple(
        element.reshape(element.shape[0], -1) for element in (grad_queries, grad_keys, grad_values)
    )


def forward_layer(source, rows, weights, vectors):
    qkv_weight, o_weight, fc1_weight, fc2_weight = weights
    ln1_gain, ln1_bias, o_bias, ln2_gain, ln2_bias, fc2_bias, q_bias, v_bias, fc1_bias = vectors
    width = source.shape[1]
    hidden = source.astype(jnp.float32)
    normed = normalize(hidden, ln1_gain, ln1_bias).astype(jnp.bfloat16)
    qkv_bias = jnp.concatenate([q_bias, jnp.zeros_like(q_bias), v_bias])
    qkv = (plain(normed, qkv_weight) + qkv_bias).astype(jnp.bfloat16)
    queries, own = qkv[:, :width], qkv[:, width:]
    both = jnp.concatenate([own, swap(own)], axis=0)
    keys, values = both[:, :width], both[:, width:]
    mixed, log_total = attend(queries, keys, values, rows)
    middle = hidden + contract_cols(mixed, o_weight) + o_bias
    normed_two = normalize(middle, ln2_gain, ln2_bias).astype(jnp.bfloat16)
    hidden_pre = plain(normed_two, fc1_weight) + fc1_bias
    active = jax.nn.gelu(hidden_pre, approximate=True).astype(jnp.bfloat16)
    result = middle + contract_cols(active, fc2_weight) + fc2_bias
    saved = (
        hidden, middle, normed, queries, keys, values, log_total, mixed, normed_two, hidden_pre,
        active,
    )
    return result.astype(jnp.bfloat16), saved


def backward_layer(grad_out, rows, weights, vectors, saved):
    qkv_weight, o_weight, fc1_weight, fc2_weight = weights
    ln1_gain, ln1_bias, o_bias, ln2_gain, ln2_bias, fc2_bias, q_bias, v_bias, fc1_bias = vectors
    (
        hidden, middle, normed, queries, keys, values, log_total, mixed, normed_two, hidden_pre,
        active,
    ) = saved
    count, width = hidden.shape
    grad_mlp = grad_out.astype(jnp.bfloat16)
    grad_fc2 = contract_rows(grad_mlp, active)
    grad_fc2_bias = jnp.sum(grad_out, axis=0)
    gelu_value, gelu_pull = jax.vjp(lambda inner: jax.nn.gelu(inner, approximate=True), hidden_pre)
    grad_pre = gelu_pull(plain(grad_mlp, fc2_weight))[0].astype(jnp.bfloat16)
    grad_fc1_bias = jnp.sum(grad_pre, axis=0, dtype=jnp.float32)
    grad_fc1 = contract_rows(normed_two, grad_pre)
    norm_value, norm_pull = jax.vjp(normalize, middle, ln2_gain, ln2_bias)
    grad_middle, grad_ln2_gain, grad_ln2_bias = norm_pull(contract_cols(grad_pre, fc1_weight))
    grad_middle = grad_middle + grad_out
    grad_o_bias = jnp.sum(grad_middle, axis=0)
    grad_branch = grad_middle.astype(jnp.bfloat16)
    grad_o = contract_rows(grad_branch, mixed)
    grad_mixed = plain(grad_branch, o_weight).astype(jnp.bfloat16)
    grad_queries, grad_keys, grad_values = attend_back(
        queries, keys, values, rows, log_total, grad_mixed
    )
    grad_both = jnp.concatenate([grad_keys, grad_values], axis=1)
    arrived = swap(grad_both[count:].astype(jnp.bfloat16))
    grad_own = grad_both[:count] + arrived.astype(jnp.float32)
    grad_qkv = jnp.concatenate([grad_queries, grad_own], axis=1).astype(jnp.bfloat16)
    grad_qkv_bias = jnp.sum(grad_qkv, axis=0, dtype=jnp.float32)
    grad_qkv_weight = contract_rows(normed, grad_qkv)
    first_value, first_pull = jax.vjp(normalize, hidden, ln1_gain, ln1_bias)
    grad_hidden, grad_ln1_gain, grad_ln1_bias = first_pull(contract_cols(grad_qkv, qkv_weight))
    grad_hidden = grad_hidden + grad_middle
    vector_terms = (
        grad_ln1_gain, grad_ln1_bias, grad_o_bias, grad_ln2_gain, grad_ln2_bias, grad_fc2_bias,
        grad_qkv_bias[:width], grad_qkv_bias[2 * width :], grad_fc1_bias,
    )
    return (
        grad_hidden.astype(jnp.bfloat16),
        vector_terms,
        (grad_qkv_weight, grad_o, grad_fc1, grad_fc2),
    )


def local(
    inputs, cotangent, lengths, ln1_gain, ln1_bias, q_weight, q_bias, k_weight, v_weight, v_bias,
    o_weight, o_bias, ln2_gain, ln2_bias, fc1_weight, fc1_bias, fc2_weight, fc2_bias,
):
    first = lax.axis_index("section") == 0
    dp, tensor = lax.axis_size("dp"), lax.axis_size("tensor")
    peers = dp * tensor
    micro_count, chunk, width = inputs.shape
    assert micro_count <= tensor
    assert tensor % 4 == 0
    depth = q_weight.shape[1]
    heads_wide = q_weight.shape[2]
    units = fc1_weight.shape[2]
    assert units == 4 * heads_wide

    def pick(own, other):
        return jnp.where(first, own, other), jnp.where(first, other, own)

    attention_block = jnp.concatenate(
        [q_weight[0], k_weight[0], v_weight[0], o_weight[0].T], axis=1
    )
    packed = jnp.stack([attention_block, fc1_weight[0], fc2_weight[0].T])
    packed = packed.reshape(3, 2, depth // 2, units)
    small = jnp.concatenate(
        [
            element.reshape(-1)
            for element in (
                ln1_gain, ln1_bias, o_bias, ln2_gain, ln2_bias, fc2_bias, q_bias, v_bias, fc1_bias,
            )
        ]
    )
    small_size = small.shape[0]
    small_rows = -(-small_size // 2048) * 16
    small = jnp.pad(small, (0, small_rows * 128 - small_size)).reshape(small_rows, 128)
    packed_layers = pick(packed, swap(packed))
    small_all = lax.all_gather(small, ALL, axis=0)
    small_layers = pick(small_all, swap(small_all))

    def gather_half(blocks):
        mine = jnp.where(first, blocks[:, 0], blocks[:, 1])
        got = lax.all_gather(mine, ALL, axis=0)
        halves = pick(got, swap(got))
        return jnp.stack(halves, axis=2).reshape(dp, tensor, blocks.shape[0], depth, units)

    def attention_weights(layer):
        blocks = gather_half(packed_layers[layer][:1])[:, :, 0]
        blocks = blocks.reshape(dp, tensor, depth, 4, heads_wide)
        qkv = blocks[:, :, :, :3].transpose(0, 2, 3, 1, 4).reshape(dp * depth, -1)
        out = blocks[:, :, :, 3].transpose(0, 2, 1, 3).reshape(dp * depth, -1)
        return qkv, out

    def mlp_weights(layer):
        blocks = gather_half(packed_layers[layer][1:])
        return tuple(
            blocks[:, :, i].transpose(0, 2, 1, 3).reshape(dp * depth, -1) for i in range(2)
        )

    slice_width = width // peers
    head_local, head_part = q_bias.shape[1], q_bias.shape[2]
    unit_rows = fc1_bias.shape[1]

    def vectors_of(layer):
        flat = small_layers[layer].reshape(peers, -1)[:, :small_size].astype(jnp.float32)
        six = [flat[:, i * slice_width : (i + 1) * slice_width].reshape(-1) for i in range(6)]
        place = 6 * slice_width
        rest = []
        for rows in (head_local, head_local, unit_rows):
            part = flat[:, place : place + rows * head_part].reshape(dp, tensor, rows, head_part)
            rest.append(part.transpose(1, 2, 0, 3).reshape(-1))
            place += rows * head_part
        return six + rest

    order = (
        [i for i in range(tensor) if i % 4 in (0, 3)],
        [i for i in range(tensor) if i % 4 in (1, 2)],
    )
    spare = tensor - micro_count
    pair = jnp.pad(jnp.stack([inputs, cotangent], axis=1), ((0, spare), (0, 0), (0, 0), (0, 0)))
    pair = lax.all_to_all(pair, "tensor", 0, 0, tiled=True)

    def own_rows(array):
        return jnp.where(
            first,
            jnp.concatenate([array[i] for i in order[0]], axis=0),
            jnp.concatenate([array[i] for i in order[1]], axis=0),
        )

    source, given = own_rows(pair[:, 0]), own_rows(pair[:, 1])

    places_two = [
        jnp.concatenate([jnp.arange(chunk, dtype=jnp.int32) + i * chunk for i in part])
        for part in order
    ]
    own_places, other_places = pick(places_two[0], places_two[1])
    micro = jnp.minimum(lax.axis_index("tensor"), micro_count - 1)
    ends = jnp.cumsum(lax.dynamic_index_in_dim(lengths[0], micro, 0, keepdims=False))
    starts = jnp.max(
        jnp.where(own_places[:, None] >= ends[None, :], ends[None, :], 0), axis=1, keepdims=True
    )
    rows = (starts, own_places[:, None], jnp.concatenate([own_places, other_places])[None, :])

    weights, vectors = [], []
    for layer in range(2):
        weights.append(attention_weights(layer) + mlp_weights(layer))
        vectors.append(vectors_of(layer))
    act_zero, saved_zero = forward_layer(source, rows, weights[0], vectors[0])
    act_one, saved_one = forward_layer(act_zero, rows, weights[1], vectors[1])

    def hand_out(zero, one):
        keep, send = pick(zero, one)
        core_zero, core_one = pick(keep, swap(send))
        pieces = [None] * tensor
        for part, array in zip(order, (core_zero, core_one)):
            for i, piece in zip(part, jnp.split(array, len(part), axis=0)):
                pieces[i] = piece
        spread = lax.all_to_all(jnp.stack(pieces), "tensor", 0, 0, tiled=True)
        return spread[:micro_count][None]

    def reduce_weights(terms):
        grad_qkv, grad_o, grad_fc1, grad_fc2 = [term.astype(jnp.bfloat16) for term in terms]
        qkv = grad_qkv.reshape(dp, depth, 3, tensor, heads_wide)
        out = grad_o.reshape(dp, depth, 1, tensor, heads_wide)
        attention = jnp.concatenate([qkv, out], axis=2).transpose(0, 3, 1, 2, 4)
        attention = attention.reshape(dp, tensor, depth, units)
        fc1 = grad_fc1.reshape(dp, depth, tensor, units).transpose(0, 2, 1, 3)
        fc2 = grad_fc2.reshape(dp, depth, tensor, units).transpose(0, 2, 1, 3)

        def scatter(blocks):
            halves = blocks.reshape(peers, 2, depth // 2, units)
            keep, send = pick(halves[:, 0], halves[:, 1])
            total = keep.astype(jnp.float32) + swap(send).astype(jnp.float32)
            total = total.astype(jnp.bfloat16)
            return lax.psum_scatter(total, ALL, scatter_dimension=0, tiled=True)[0]

        return jnp.stack([scatter(fc2), scatter(fc1), scatter(attention)])

    def small_terms(terms):
        flat = [term.reshape(peers, -1) for term in terms[:6]]
        for term in terms[6:]:
            part = term.reshape(tensor, -1, dp, head_part).transpose(2, 0, 1, 3)
            flat.append(part.reshape(peers, -1))
        flat = jnp.concatenate(flat, axis=1)
        return jnp.pad(flat, ((0, 0), (0, small_rows * 128 - small_size)))

    grad_one = given.astype(jnp.float32)
    back_one, small_one, large_one = backward_layer(
        grad_one, rows, weights[1], vectors[1], saved_one
    )
    shard_one = reduce_weights(large_one)
    back_zero, small_zero, large_zero = backward_layer(
        back_one.astype(jnp.float32), rows, weights[0], vectors[0], saved_zero
    )
    shard_zero = reduce_weights(large_zero)
    acts = hand_out(act_zero, act_one)
    backs = hand_out(back_zero, back_one)

    keep, send = pick(small_terms(small_zero), small_terms(small_one))
    small_sum = (keep + swap(send)).reshape(peers, small_rows, 128)
    small_sum = lax.psum_scatter(small_sum, ALL, scatter_dimension=0, tiled=True)
    small_sum = small_sum.reshape(-1)[:small_size]
    keep, send = pick(shard_zero, shard_one)
    halves = pick(keep, swap(send))
    shard = jnp.concatenate(halves, axis=1).astype(jnp.float32)
    grad_fc2 = shard[0].T
    grad_fc1 = shard[1]
    grad_q, grad_k, grad_v, grad_o = jnp.split(shard[2], 4, axis=1)
    grad_o = grad_o.T
    six = [small_sum[i * slice_width : (i + 1) * slice_width][None] for i in range(6)]
    place = 6 * slice_width
    rest = []
    for count in (head_local, head_local, unit_rows):
        part = small_sum[place : place + count * head_part]
        rest.append(part.reshape(1, count, head_part))
        place += count * head_part
    return (
        acts, backs, six[0], six[1], grad_q[None], rest[0], grad_k[None], grad_v[None], rest[1],
        grad_o[None], six[2], six[3], six[4], grad_fc1[None], rest[2], grad_fc2[None], six[5],
    )


def solution(mesh):
    return jax.shard_map(
        local,
        mesh=mesh,
        in_specs=(
            P(None, ("dp", "tensor"), None),
            P(None, ("dp", "tensor"), None),
            P("dp", None, None),
            P("section", ("dp", "tensor")),
            P("section", ("dp", "tensor")),
            P("section", "dp", "tensor"),
            P("section", "tensor", "dp"),
            P("section", "dp", "tensor"),
            P("section", "dp", "tensor"),
            P("section", "tensor", "dp"),
            P("section", "tensor", "dp"),
            P("section", ("dp", "tensor")),
            P("section", ("dp", "tensor")),
            P("section", ("dp", "tensor")),
            P("section", "dp", "tensor"),
            P("section", "tensor", "dp"),
            P("section", "tensor", "dp"),
            P("section", ("dp", "tensor")),
        ),
        out_specs=(
            P("section", None, ("dp", "tensor"), None),
            P("section", None, ("dp", "tensor"), None),
            P("section", ("dp", "tensor")),
            P("section", ("dp", "tensor")),
            P("section", "dp", "tensor"),
            P("section", "tensor", "dp"),
            P("section", "dp", "tensor"),
            P("section", "dp", "tensor"),
            P("section", "tensor", "dp"),
            P("section", "tensor", "dp"),
            P("section", ("dp", "tensor")),
            P("section", ("dp", "tensor")),
            P("section", ("dp", "tensor")),
            P("section", "dp", "tensor"),
            P("section", "tensor", "dp"),
            P("section", "tensor", "dp"),
            P("section", ("dp", "tensor")),
        ),
        check_vma=False,
    )
```

time: 2970 us -> 1700 us (0.57)
  waiting for transfers between devices: 2040 us -> 651 us
  local copies, waits for them, and re-layouts: 98.2 us -> 403 us
  matrix products: 406 us -> 299 us
  blocking collectives: 178 us -> 74.3 us
    unnamed x63 -> x11, waiting for transfers between devices: 877 us -> 0.18 us
    all_gather x18 -> x4, waiting for transfers between devices: 469 us -> 8.73 us  [gather_half(): got = lax.all_gather(mine, ALL, axis=0)]
    reshape x0 -> x66, local copies, waits for them, and re-layouts: none -> 180 us  [the longest x4 29.9 us: reduce_weights(): qkv = grad_qkv.reshape(dp, depth, 3, tensor, heads_wide)]
    reduce_scatter x17 -> x7, waiting for transfers between devices: 683 us -> 602 us  [the longest x6 602 us: scatter(): return lax.psum_scatter(total, ALL, scatter_dimension=0, tiled=True)[0]]
    unnamed x1 -> x0, blocking collectives: 78.6 us -> none
    transpose x0 -> x27, local copies, waits for them, and re-layouts: none -> 65.7 us  [the longest x4 26.7 us: attention_weights(): qkv = blocks[:, :, :, :3].transpose(0, 2, 3, 1, 4).reshape(dp * depth, -1)]
    another operation x1 -> x16, local copies, waits for them, and re-layouts: 1.36 us -> 65.3 us  [the longest x2 26.1 us: attention_weights(): blocks = blocks.reshape(dp, tensor, depth, 4, heads_wide)]
    unnamed x582 -> x345, local copies, waits for them, and re-layouts: 85.5 us -> 25.8 us
  transfers between devices with their start and end apart: 55 -> 34, of which waited for: 50 -> 13; matrix products, arithmetic and copies ran while one was open for 7% -> 37% of each run, Pallas kernels for 0% -> 0%
where the time goes in v1:
time: 1700 us; the launch traced here: 1690 us
  waiting for transfers between devices  651 us (38%)
  local copies, waits for them, and re-layouts  403 us (24%)
  matrix products  299 us (18%)
  other arithmetic  225 us (13%)
  blocking collectives  74.3 us (4%)
  starting transfers between devices  19.4 us (1%)
    reduce_scatter x6, waiting for transfers between devices, scatter(): return lax.psum_scatter(total, ALL, scatter_dimension=0, tiled=True)[0]  602 us
    all_gather x1, blocking collectives, local(): small_all = lax.all_gather(small, ALL, axis=0)  74.3 us
    convert_element_type x2, other arithmetic, attend_back(): grad_scores = (probs * (grad_probs - row_delta)).astype(jnp.bfloat16)  53.4 us
    dot_general x8, matrix products, contract_rows(): lax.dot_general(left, right, (((0,), (0,)), ((), ())), preferred_element_...  52.6 us
    dot_general x2, matrix products, attend_back(): jnp.einsum('qhd,khd->hqk', grads, heads_of(values), preferred_element_typ...  49.1 us
    another operation x8, other arithmetic, gather_half(): jnp.stack(halves, axis=2).reshape(dp, tensor, blocks.shape[0], depth, units)  35.9 us
    dot_general x8, matrix products, plain(): return jnp.dot(left, right, preferred_element_type=jnp.float32)  34.3 us
  transfers between devices with their start and end apart: 34, of which 13 were waited for; matrix products, arithmetic and copies ran while one was open for 37% of the time, Pallas kernels for 0%

profile of v1, /device:TPU:0, one launch (start us, length us, event | category | flops | bytes accessed | tf_op | source)
XLA Modules:
  0.0 1688.4 jit_solution(2731283454239321009)
XLA Ops:
  31.4 74.3 %all_gather.19 = bf16[16,16,128]{2,1,0:T(8,128)(2,1)} all-gather(bf16[1,16,128]{2,1,0:T(8,128)(2,1)S(1)} %pad_bitcast_fusion), channel_id=1, replica_groups=mesh['section'=2,'dp'=4,'tensor'=4] {'dp','tensor'}, dimensions={0}, use_global_device_ids=true | all-gather | bytes 69632 | tf_op jit(solution)/shard_map/all_gather | solution.py:191
  171.1 13.1 reshape_squeeze_reshape.6
  230.2 12.9 reshape_squeeze_reshape.7
  289.0 14.8 fusion.113
  304.4 14.8 fusion
  319.6 14.1 fusion.72
  433.8 14.2 fusion.115
  448.0 14.8 fusion.1
  462.9 13.6 fusion.71
  501.8 14.5 fusion.4
  516.4 24.9 %multiply_reduce_fusion.1 = (f32[12,576]{1,0:T(8,128)}, f32[12,576,1152]{2,1,0:T(8,128)}) fusion(f32[12,576,1152]{2,1,0:T(8,128)} %get-tuple-element.204, f32[12,576]{1,0:T(8,128)S(1)} %log_add_fusion, bf16[576,12,64]{0,2,1:T(8,128)(2,1)S(1)} %bitcast.432, bf16[1152,12,64]{0,2,1:T(8,128)(2,1)S(1)} %bitcast.438), kind=kOutput, calls=%fused_computation.3 | convolution fusion | flops 1043096832 | bytes 66410496 | tf_op jit(solution)/shard_map/qhd,khd->hqk/dot_general | solution.py:64
  544.6 26.8 %multiply_convert_fusion.1 = bf16[12,576,1152]{2,1,0:T(8,128)(2,1)} fusion(f32[12,576,1152]{2,1,0:T(8,128)} %get-tuple-element.211, f32[12,576,1152]{2,1,0:T(8,128)} %get-tuple-element.204, f32[12,576]{1,0:T(8,128)} %get-tuple-element.210, f32[12,576]{1,0:T(8,128)} %copy-done.67), kind=kLoop, calls=%fused_computation.2 | loop fusion | flops 31850496 | bytes 79681536 | tf_op jit(solution)/shard_map/convert_element_type | solution.py:71
  660.5 15.1 fusion.6
  675.6 24.2 %multiply_reduce_fusion = (f32[12,576]{1,0:T(8,128)S(1)}, f32[12,576,1152]{2,1,0:T(8,128)}) fusion(f32[12,576,1152]{2,1,0:T(8,128)} %get-tuple-element.198, f32[12,576]{1,0:T(8,128)S(1)} %copy-done.66, bf16[576,12,64]{0,2,1:T(8,128)(2,1)S(1)} %bitcast.434, bf16[1152,12,64]{0,2,1:T(8,128)(2,1)S(1)} %bitcast.436), kind=kOutput, calls=%fused_computation.1 | convolution fusion | flops 1043096832 | bytes 66410496 | tf_op jit(solution)/shard_map/qhd,khd->hqk/dot_general | solution.py:64
  705.0 26.5 %multiply_convert_fusion = bf16[12,576,1152]{2,1,0:T(8,128)(2,1)} fusion(f32[12,576,1152]{2,1,0:T(8,128)} %get-tuple-element.215, f32[12,576,1152]{2,1,0:T(8,128)} %get-tuple-element.198, f32[12,576]{1,0:T(8,128)S(1)} %get-tuple-element.214, f32[12,576]{1,0:T(8,128)S(1)} %copy-done.66), kind=kLoop, calls=%fused_computation | loop fusion | flops 31850496 | bytes 79681536 | tf_op jit(solution)/shard_map/convert_element_type | solution.py:71
  763.0 11.9 multiply_convert_fusion.4
  929.0 11.8 reshape_reshape.7
  995.1 11.8 reshape_reshape.6
  1041.1 19.7 %all-to-all-done.1 = bf16[4,288,768]{2,1,0:T(8,128)(2,1)S(1)} async-done(((bf16[4,288,768]{2,1,0:T(8,128)(2,1)}), bf16[4,288,768]{2,1,0:T(8,128)(2,1)S(1)}, u32[]{:S(2)}, u32[]{:S(2)}) %all-to-all-start.1) | async-done | bytes 1769504 | tf_op jit(solution)/shard_map/all_to_all | solution.py:271
  1067.2 74.6 %reduce-scatter.18.cloned.1.call-done = bf16[1,96,768]{2,1,0:T(8,128)(2,1)} async-done(((bf16[16,96,768]{2,1,0:T(8,128)(2,1)}), bf16[1,96,768]{2,1,0:T(8,128)(2,1)}) %reduce-scatter.18.cloned.1.call-update) | async-done | bytes 147472 | tf_op jit(solution)/shard_map/reduce_scatter | solution.py:288
  1142.7 132.2 %reduce-scatter.10.cloned.1.call-done = bf16[1,96,768]{2,1,0:T(8,128)(2,1)} async-done(((bf16[16,96,768]{2,1,0:T(8,128)(2,1)}), bf16[1,96,768]{2,1,0:T(8,128)(2,1)}) %reduce-scatter.10.cloned.1.call-update) | async-done | bytes 147472 | tf_op jit(solution)/shard_map/reduce_scatter | solution.py:288
  1275.8 131.6 %reduce-scatter.12.cloned.1.call-done = bf16[1,96,768]{2,1,0:T(8,128)(2,1)} async-done(((bf16[16,96,768]{2,1,0:T(8,128)(2,1)}), bf16[1,96,768]{2,1,0:T(8,128)(2,1)}) %reduce-scatter.12.cloned.1.call-update) | async-done | bytes 147472 | tf_op jit(solution)/shard_map/reduce_scatter | solution.py:288
  1408.3 132.2 %reduce-scatter.20.cloned.1.call-done = bf16[1,96,768]{2,1,0:T(8,128)(2,1)} async-done(((bf16[16,96,768]{2,1,0:T(8,128)(2,1)}), bf16[1,96,768]{2,1,0:T(8,128)(2,1)}) %reduce-scatter.20.cloned.1.call-update) | async-done | bytes 147472 | tf_op jit(solution)/shard_map/reduce_scatter | solution.py:288
  1541.4 131.7 %reduce-scatter.14.cloned.1.call-done = bf16[1,96,768]{2,1,0:T(8,128)(2,1)} async-done(((bf16[16,96,768]{2,1,0:T(8,128)(2,1)}), bf16[1,96,768]{2,1,0:T(8,128)(2,1)}) %reduce-scatter.14.cloned.1.call-update) | async-done | bytes 147472 | tf_op jit(solution)/shard_map/reduce_scatter | solution.py:288
  (692 shorter events, 695.6 us)
Async XLA Ops:
  7.2 100.2 %all-gather.7.cloned.1.call-start = ((), (), s32[]{:S(2)}) async-start(), calls=%async_computation.10 | async-start | bytes 2506752 | tf_op jit(solution)/shard_map/all_gather | solution.py:196
  14.8 151.2 %all-gather.9.cloned.1.call-start = ((), (), s32[]{:S(2)}) async-start(), calls=%async_computation.11 | async-start | bytes 2506752 | tf_op jit(solution)/shard_map/all_gather | solution.py:196
  15.6 303.6 %all-gather.11.cloned.1.call-start = ((), (), s32[]{:S(2)}) async-start(), calls=%async_computation.19 | async-start | bytes 5013504 | tf_op jit(solution)/shard_map/all_gather | solution.py:196
  19.5 134.9 %all-to-all-start = ((bf16[4,2,288,768]{3,2,1,0:T(8,128)(2,1)}), bf16[4,2,288,768]{3,2,1,0:T(8,128)(2,1)S(1)}, u32[]{:S(2)}, u32[]{:S(2)}) async-start(bf16[4,2,288,768]{3,2,1,0:T(8,128)(2,1)} %fusion.40), calls=%async_computation | async-start | bytes 7077888 | tf_op jit(solution)/shard_map/all_to_all | solution.py:234
  24.7 314.5 %all-gather.13.cloned.1.call-start = ((), (), s32[]{:S(2)}) async-start(), calls=%async_computation.20 | async-start | bytes 5013504 | tf_op jit(solution)/shard_map/all_gather | solution.py:196
  107.4 58.7 %collective-permute-start.2 = (bf16[16,1,96,768]{3,2,0,1:T(8,128)(2,1)}, bf16[16,1,96,768]{3,2,0,1:T(8,128)(2,1)}, u32[]{:S(2)}, u32[]{:S(2)}) collective-permute-start(bf16[16,1,96,768]{3,2,0,1:T(8,128)(2,1)} %bitcast.470), channel_id=1, source_target_pairs={{0,16},{16,0},{1,17},{17,1},{2,18},{18,2},{3,19},{19,3},{4,20},{20... | collective-permute-start | bytes 7077896 | tf_op jit(solution)/shard_map/ppermute | solution.py:13
  166.1 59.1 %collective-permute-start.5 = (bf16[16,1,96,768]{3,2,0,1:T(8,128)(2,1)}, bf16[16,1,96,768]{3,2,0,1:T(8,128)(2,1)}, u32[]{:S(2)}, u32[]{:S(2)}) collective-permute-start(bf16[16,1,96,768]{3,2,0,1:T(8,128)(2,1)} %bitcast.469), channel_id=1, source_target_pairs={{0,16},{16,0},{1,17},{17,1},{2,18},{18,2},{3,19},{19,3},{4,20},{20... | collective-permute-start | bytes 7077896 | tf_op jit(solution)/shard_map/ppermute | solution.py:13
  212.8 68.5 %collective-permute-start.3 = (bf16[576,1536]{1,0:T(8,128)(2,1)}, bf16[576,1536]{1,0:T(8,128)(2,1)}, u32[]{:S(2)}, u32[]{:S(2)}) collective-permute-start(bf16[576,1536]{1,0:T(8,128)(2,1)} %slice.430), channel_id=1, source_target_pairs={{0,16},{16,0},{1,17},{17,1},{2,18},{18,2},{3,19},{19,3},{4,20},{20... | collective-permute-start | bytes 5308424 | tf_op jit(solution)/shard_map/ppermute | solution.py:13
  214.0 851.5 %reduce-scatter.8.cloned.1.call-start = ((), (), s32[]{:S(2)}) async-start(), calls=%async_computation.12 | async-start | bytes 139264 | tf_op jit(solution)/shard_map/reduce_scatter | solution.py:314
  319.2 20.1 %collective-permute-start.4 = (bf16[16,2,96,768]{3,2,1,0:T(8,128)(2,1)}, bf16[16,2,96,768]{3,2,1,0:T(8,128)(2,1)}, u32[]{:S(2)}, u32[]{:S(2)}) collective-permute-start(bf16[16,2,96,768]{3,2,1,0:T(8,128)(2,1)} %bitcast.461), channel_id=1, source_target_pairs={{0,16},{16,0},{1,17},{17,1},{2,18},{18,2},{3,19},{19,3},{4,20},{20... | collective-permute-start | bytes 14155784 | tf_op jit(solution)/shard_map/ppermute | solution.py:13
  339.2 44.1 %collective-permute-start.7 = (bf16[16,2,96,768]{3,2,1,0:T(8,128)(2,1)}, bf16[16,2,96,768]{3,2,1,0:T(8,128)(2,1)}, u32[]{:S(2)}, u32[]{:S(2)}) collective-permute-start(bf16[16,2,96,768]{3,2,1,0:T(8,128)(2,1)} %bitcast.463), channel_id=1, source_target_pairs={{0,16},{16,0},{1,17},{17,1},{2,18},{18,2},{3,19},{19,3},{4,20},{20... | collective-permute-start | bytes 14155784 | tf_op jit(solution)/shard_map/ppermute | solution.py:13
  382.9 43.2 %collective-permute-start.6 = (bf16[576,1536]{1,0:T(8,128)(2,1)}, bf16[576,1536]{1,0:T(8,128)(2,1)}, u32[]{:S(2)}, u32[]{:S(2)}) collective-permute-start(bf16[576,1536]{1,0:T(8,128)(2,1)} %slice.452), channel_id=1, source_target_pairs={{0,16},{16,0},{1,17},{17,1},{2,18},{18,2},{3,19},{19,3},{4,20},{20... | collective-permute-start | bytes 5308424 | tf_op jit(solution)/shard_map/ppermute | solution.py:13
  589.8 44.9 %collective-permute-start.9 = (bf16[576,1536]{1,0:T(8,128)(2,1)}, bf16[576,1536]{1,0:T(8,128)(2,1)}, u32[]{:S(2)}, u32[]{:S(2)}) collective-permute-start(bf16[576,1536]{1,0:T(8,128)(2,1)} %fusion.42), channel_id=1, source_target_pairs={{0,16},{16,0},{1,17},{17,1},{2,18},{18,2},{3,19},{19,3},{4,20},{20... | collective-permute-start | bytes 5308424 | tf_op jit(solution)/shard_map/ppermute | solution.py:13
  751.0 27.6 %collective-permute-start.10 = (bf16[576,1536]{1,0:T(8,128)(2,1)}, bf16[576,1536]{1,0:T(8,128)(2,1)}, u32[]{:S(2)}, u32[]{:S(2)}) collective-permute-start(bf16[576,1536]{1,0:T(8,128)(2,1)} %fusion.41), channel_id=1, source_target_pairs={{0,16},{16,0},{1,17},{17,1},{2,18},{18,2},{3,19},{19,3},{4,20},{20... | collective-permute-start | bytes 5308424 | tf_op jit(solution)/shard_map/ppermute | solution.py:13
  753.1 41.0 %collective-permute-start.16 = (bf16[16,96,768]{2,1,0:T(8,128)(2,1)}, bf16[16,96,768]{2,1,0:T(8,128)(2,1)}, u32[]{:S(2)}, u32[]{:S(2)}) collective-permute-start(bf16[16,96,768]{2,1,0:T(8,128)(2,1)} %select_bitcast_fusion.6), channel_id=1, source_target_pairs={{0,16},{16,0},{1,17},{17,1},{2,18},{18,2},{3,19},{19,3},{4,20},{20... | collective-permute-start | bytes 7077896 | tf_op jit(solution)/shard_map/ppermute | solution.py:13
  794.0 272.2 %reduce-scatter.16.cloned.1.call-start = ((), (), s32[]{:S(2)}) async-start(), calls=%async_computation.16 | async-start | bytes 2506752 | tf_op jit(solution)/shard_map/reduce_scatter | solution.py:288
  799.8 342.0 %reduce-scatter.18.cloned.1.call-start = ((), (), s32[]{:S(2)}) async-start(), calls=%async_computation.17 | async-start | bytes 2506752 | tf_op jit(solution)/shard_map/reduce_scatter | solution.py:288
  828.5 446.4 %reduce-scatter.10.cloned.1.call-start = ((), (), s32[]{:S(2)}) async-start(), calls=%async_computation.13 | async-start | bytes 2506752 | tf_op jit(solution)/shard_map/reduce_scatter | solution.py:288
  858.6 548.8 %reduce-scatter.12.cloned.1.call-start = ((), (), s32[]{:S(2)}) async-start(), calls=%async_computation.14 | async-start | bytes 2506752 | tf_op jit(solution)/shard_map/reduce_scatter | solution.py:288
  886.9 653.6 %reduce-scatter.20.cloned.1.call-start = ((), (), s32[]{:S(2)}) async-start(), calls=%async_computation.18 | async-start | bytes 2506752 | tf_op jit(solution)/shard_map/reduce_scatter | solution.py:288
  950.8 722.4 %reduce-scatter.14.cloned.1.call-start = ((), (), s32[]{:S(2)}) async-start(), calls=%async_computation.15 | async-start | bytes 2506752 | tf_op jit(solution)/shard_map/reduce_scatter | solution.py:288
  1011.0 11.5 collective-permute-start.15
  1033.2 27.6 %all-to-all-start.1 = ((bf16[4,288,768]{2,1,0:T(8,128)(2,1)}), bf16[4,288,768]{2,1,0:T(8,128)(2,1)S(1)}, u32[]{:S(2)}, u32[]{:S(2)}) async-start(bf16[4,288,768]{2,1,0:T(8,128)(2,1)} %pad_maximum_fusion.10), calls=%async_computation.1 | async-start | bytes 3538944 | tf_op jit(solution)/shard_map/all_to_all | solution.py:271
  1060.8 616.7 %all-to-all-start.2 = ((bf16[4,288,768]{2,1,0:T(8,128)(2,1)}), bf16[4,288,768]{2,1,0:T(8,128)(2,1)S(1)}, u32[]{:S(2)}, u32[]{:S(2)}) async-start(bf16[4,288,768]{2,1,0:T(8,128)(2,1)} %pad_maximum_fusion.11), calls=%async_computation.2 | async-start | bytes 3538944 | tf_op jit(solution)/shard_map/all_to_all | solution.py:271
  (178 other events, 2481.9 us)
Sparse Core Ops, SparseCore 0:
  15.0 86.3 all-gather.6
  104.7 61.3 all-gather.8
  168.9 79.2 all-gather.10
  250.8 79.0 all-gather.12
  794.1 75.0 reduce-scatter.7
  874.7 124.7 reduce-scatter.15
  1004.4 137.3 reduce-scatter.17
  1147.5 127.3 reduce-scatter.9
  1279.8 127.5 reduce-scatter.11
  1412.9 127.5 reduce-scatter.19
  1545.4 127.6 reduce-scatter.13
